TPU v7x, 512 devices: a whole 4x4x16 slice. The times are simulated.
512 devices in a mesh: ctx: 64 (over z_lo, y, core), ch: 8 (over z_hi, x).
Axes of the slice: x: 4, y: 4, z: 16 (z_hi: 2, z_lo: 8; z = z_hi * 8 + z_lo), core: 2. Of those that a mesh axis runs over, the one named last changes fastest.
Arguments:
- queries: bfloat16 [8192, 4096], P('ctx', 'ch'), may hold values from -6 to 6
- keys: bfloat16 [8192, 4096], P('ctx', 'ch'), may hold values from -6 to 6
- values: bfloat16 [8192, 4096], P('ctx', 'ch'), may hold values from -6 to 6
- conv_out: bfloat16 [8192, 4096], P('ctx', 'ch'), may hold values from -6 to 6
- filters: bfloat16 [8192, 4096], P('ctx', 'ch'), may hold values from -1.2 to 1.2
- out_grad: bfloat16 [8192, 4096], P('ctx', 'ch'), may hold values from -16 to 16
- out_weight: bfloat16 [4096, 4096], P('ctx', 'ch'), may hold values from -0.09375 to 0.09375
- moment_one: float32 [4096, 4096], P('ctx', 'ch'), may hold values from -64 to 64
- moment_two: float32 [4096, 4096], P('ctx', 'ch'), may hold values from 200 to 2000
Outputs:
- query_grad: bfloat16 [8192, 4096], P('ctx', 'ch')
- key_grad: bfloat16 [8192, 4096], P('ctx', 'ch')
- value_grad: bfloat16 [8192, 4096], P('ctx', 'ch')
- filter_grad: bfloat16 [8192, 4096], P('ctx', 'ch')
- new_weight: bfloat16 [4096, 4096], P('ctx', 'ch')
- new_moment_one: float32 [4096, 4096], P('ctx', 'ch')
- new_moment_two: float32 [4096, 4096], P('ctx', 'ch')
All inputs are finite; a program needn't handle non-finite values.
Results may differ from a plain program's by a relative error of at most 0.0058.
Values may be sent and summed in bfloat16 or wider, within the bound.
A program may use at most 64 MiB of HBM per device.

v0:
```python
import math

import jax
import jax.numpy as jnp
from jax import lax
from jax.sharding import PartitionSpec as P

BETA_ONE = 0.9
BETA_TWO = 0.95
STEP_RATE = 0.003
DECAY = 0.1
ADAM_STABILIZER = 1e-08


def angle_table(rows, cols, period):
    product = lax.broadcasted_iota(jnp.int32, (rows, cols), 0) * lax.broadcasted_iota(
        jnp.int32, (rows, cols), 1
    )
    angle = (product % period).astype(jnp.float32) * (2.0 * math.pi / period)
    return (jnp.cos(angle), jnp.sin(angle))


def mixing(left, table, form):
    return jnp.einsum(
        form, left, table, precision=lax.Precision.HIGHEST, preferred_element_type=jnp.float32
    )


def make_tables(length):
    span = 128
    radix = 2 * length // span
    cos_outer, sin_outer = angle_table(radix, radix, radix)
    cos_inner, sin_inner = angle_table(span, span, span)
    twist_cos, twist_sin = angle_table(radix, span, radix * span)
    return (cos_outer, sin_outer, cos_inner, sin_inner, twist_cos, twist_sin)


def spectrum(signal, tables):
    cos_outer, sin_outer, cos_inner, sin_inner, twist_cos, twist_sin = tables
    radix = cos_outer.shape[0]
    span = cos_inner.shape[0]
    lower = signal.reshape(signal.shape[0], radix // 2, span)
    first_real = mixing(lower, cos_outer[: radix // 2], "cjm,jk->ckm")
    first_imag = -mixing(lower, sin_outer[: radix // 2], "cjm,jk->ckm")
    turned_real = first_real * twist_cos + first_imag * twist_sin
    turned_imag = first_imag * twist_cos - first_real * twist_sin
    out_real = mixing(turned_real, cos_inner, "ckm,ml->ckl") + mixing(
        turned_imag, sin_inner, "ckm,ml->ckl"
    )
    out_imag = mixing(turned_imag, cos_inner, "ckm,ml->ckl") - mixing(
        turned_real, sin_inner, "ckm,ml->ckl"
    )
    return (out_real, out_imag)


def inverse_half(spec_real, spec_imag, tables):
    cos_outer, sin_outer, cos_inner, sin_inner, twist_cos, twist_sin = tables
    radix = cos_outer.shape[0]
    span = cos_inner.shape[0]
    back_real = mixing(spec_real, cos_inner, "ckl,lm->ckm") - mixing(
        spec_imag, sin_inner, "ckl,lm->ckm"
    )
    back_imag = mixing(spec_real, sin_inner, "ckl,lm->ckm") + mixing(
        spec_imag, cos_inner, "ckl,lm->ckm"
    )
    turned_real = back_real * twist_cos - back_imag * twist_sin
    turned_imag = back_real * twist_sin + back_imag * twist_cos
    signal = mixing(turned_real, cos_outer[:, : radix // 2], "ckm,kj->cjm") - mixing(
        turned_imag, sin_outer[:, : radix // 2], "ckm,kj->cjm"
    )
    return signal.reshape(signal.shape[0], -1) / (radix * span)


def on_device(
    queries, keys, values, conv_out, filters, out_grad, out_weight, moment_one, moment_two
):
    grad_full = lax.all_gather(out_grad, "ch", axis=1, tiled=True)
    query_float = queries.astype(jnp.float32)
    convolved_single = conv_out.astype(jnp.float32)
    proj_in = (query_float * convolved_single).astype(jnp.bfloat16)
    key_value = (keys.astype(jnp.float32) * values.astype(jnp.float32)).astype(jnp.bfloat16)
    out_delta = jnp.dot(
        grad_full,
        lax.all_gather(out_weight, "ctx", axis=0, tiled=True),
        preferred_element_type=jnp.float32,
    )
    query_grad = (out_delta * convolved_single).astype(jnp.bfloat16)
    conv_grad = (out_delta * query_float).astype(jnp.bfloat16)
    grad_chan, pair_chan, filt_chan = (
        lax.all_to_all(conv_grad.T, "ctx", split_axis=0, concat_axis=1, tiled=True),
        lax.all_to_all(key_value.T, "ctx", split_axis=0, concat_axis=1, tiled=True),
        lax.all_to_all(filters.T, "ctx", split_axis=0, concat_axis=1, tiled=True),
    )
    tables = make_tables(grad_chan.shape[1])
    grad_real, grad_imag = spectrum(grad_chan.astype(jnp.float32), tables)
    filt_real, filt_imag = spectrum(filt_chan.astype(jnp.float32), tables)
    pair_real, pair_imag = spectrum(pair_chan.astype(jnp.float32), tables)
    delta_chan = inverse_half(
        filt_real * grad_real + filt_imag * grad_imag,
        filt_real * grad_imag - filt_imag * grad_real,
        tables,
    ).astype(jnp.bfloat16)
    filt_grad_chan = inverse_half(
        pair_real * grad_real + pair_imag * grad_imag,
        pair_real * grad_imag - pair_imag * grad_real,
        tables,
    ).astype(jnp.bfloat16)
    returned_delta, filt_back = (
        lax.all_to_all(delta_chan, "ctx", split_axis=1, concat_axis=0, tiled=True),
        lax.all_to_all(filt_grad_chan, "ctx", split_axis=1, concat_axis=0, tiled=True),
    )
    value_delta = returned_delta.T.astype(jnp.float32)
    filter_grad = filt_back.T
    key_grad = (value_delta * values.astype(jnp.float32)).astype(jnp.bfloat16)
    value_grad = (value_delta * keys.astype(jnp.float32)).astype(jnp.bfloat16)
    grad_owned = lax.all_to_all(grad_full, "ctx", split_axis=1, concat_axis=0, tiled=True)
    weight_grad = lax.dot_general(
        grad_owned,
        lax.all_gather(proj_in, "ctx", axis=0, tiled=True),
        (((0,), (0,)), ((), ())),
        preferred_element_type=jnp.float32,
    )
    new_moment_one = BETA_ONE * moment_one + (1.0 - BETA_ONE) * weight_grad
    new_moment_two = BETA_TWO * moment_two + (1.0 - BETA_TWO) * weight_grad * weight_grad
    corr_one = 1.0 - BETA_ONE**10
    corr_two = 1.0 - BETA_TWO**10
    weight_float = out_weight.astype(jnp.float32)
    update = new_moment_one / corr_one / (jnp.sqrt(new_moment_two / corr_two) + ADAM_STABILIZER)
    new_weight = (weight_float - STEP_RATE * (update + DECAY * weight_float)).astype(jnp.bfloat16)
    return (
        query_grad,
        key_grad,
        value_grad,
        filter_grad,
        new_weight,
        new_moment_one,
        new_moment_two,
    )


def solution(mesh):
    return jax.shard_map(
        on_device,
        mesh=mesh,
        in_specs=(
            P("ctx", "ch"),
            P("ctx", "ch"),
            P("ctx", "ch"),
            P("ctx", "ch"),
            P("ctx", "ch"),
            P("ctx", "ch"),
            P("ctx", "ch"),
            P("ctx", "ch"),
            P("ctx", "ch"),
        ),
        out_specs=(
            P("ctx", "ch"),
            P("ctx", "ch"),
            P("ctx", "ch"),
            P("ctx", "ch"),
            P("ctx", "ch"),
            P("ctx", "ch"),
            P("ctx", "ch"),
        ),
        check_vma=False,
    )
```

profile of v0, /device:TPU:7, one launch (start us, length us, event | category | flops | bytes accessed | tf_op | source)
XLA Modules:
  0.0 425.1 jit_solution(11557473315128766959)
XLA Ops:
  7.2 0.0 all-gather.4.cloned.1.call-start
  7.2 1.7 copy.39
  8.9 0.0 all-gather.6.cloned.1.call-start
  8.9 0.7 all-gather.6.cloned.1.call-update
  9.7 0.0 all-gather.8.cloned.1.call-start
  9.7 95.7 %all-gather.4.cloned.1.call-done = bf16[128,4096]{0,1:T(8,128)(2,1)} async-done(((bf16[128,512]{0,1:T(8,128)(2,1)}), bf16[128,4096]{0,1:T(8,128)(2,1)}) %all-gather.4.cloned.1.call-update) | async-done | bytes 1048592 | tf_op jit(solution)/shard_map/all_gather | solution.py:77
  105.4 118.0 %all-gather.6.cloned.1.call-done = bf16[4096,512]{1,0:T(8,128)(2,1)} async-done(((bf16[64,512]{1,0:T(8,128)(2,1)}), bf16[4096,512]{1,0:T(8,128)(2,1)}) %all-gather.6.cloned.1.call-update) | async-done | bytes 4194320 | tf_op jit(solution)/shard_map/all_gather | solution.py:84
  223.5 4.0 fusion.59
  227.5 1.0 copy.48
  228.5 1.0 copy.47
  229.6 0.7 fusion.58
  230.3 7.4 %all-to-all-start.3 = ((bf16[64,8,128]{2,1,0:T(8,128)(2,1)}), bf16[64,8,128]{2,1,0:T(8,128)(2,1)S(1)}, u32[]{:S(2)}, u32[]{:S(2)}) async-start(bf16[64,8,128]{2,1,0:T(8,128)(2,1)} %fusion.58), calls=%async_computation.3 | async-start | bytes 262144 | tf_op jit(solution)/shard_map/all_to_all | solution.py:91
  237.7 1.7 copy.40
  239.3 0.3 fusion.112
  239.6 0.3 fusion.110
  239.9 13.3 %all-to-all-done.3 = bf16[64,8,128]{2,1,0:T(8,128)(2,1)S(1)} async-done(((bf16[64,8,128]{2,1,0:T(8,128)(2,1)}), bf16[64,8,128]{2,1,0:T(8,128)(2,1)S(1)}, u32[]{:S(2)}, u32[]{:S(2)}) %all-to-all-start.3) | async-done | bytes 131104 | tf_op jit(solution)/shard_map/all_to_all | solution.py:91
  253.2 5.3 %all-to-all-start = ((bf16[64,8,128]{2,1,0:T(8,128)(2,1)}), bf16[64,8,128]{2,1,0:T(8,128)(2,1)S(1)}, u32[]{:S(2)}, u32[]{:S(2)}) async-start(bf16[64,8,128]{2,1,0:T(8,128)(2,1)} %bitcast.3), calls=%async_computation | async-start | bytes 262144 | tf_op jit(solution)/shard_map/all_to_all | solution.py:92
  258.5 0.3 fusion.113
  258.7 0.4 convolution_negate_fusion
  259.2 0.4 fusion.61
  259.6 15.0 %all-to-all-done = bf16[64,8,128]{2,1,0:T(8,128)(2,1)S(1)} async-done(((bf16[64,8,128]{2,1,0:T(8,128)(2,1)}), bf16[64,8,128]{2,1,0:T(8,128)(2,1)S(1)}, u32[]{:S(2)}, u32[]{:S(2)}) %all-to-all-start) | async-done | bytes 131104 | tf_op jit(solution)/shard_map/all_to_all | solution.py:92
  274.6 0.4 fusion.67
  275.0 0.4 convolution_negate_fusion.2
  275.5 0.8 fusion.20
  276.3 1.6 fusion.24
  277.9 0.8 fusion.12
  278.7 0.8 convolution_add_fusion.1
  279.6 0.8 convolution_subtract_fusion.4
  280.4 1.7 copy.42
  282.1 5.2 %all-to-all-start.1 = ((bf16[64,8,128]{2,1,0:T(8,128)(2,1)}), bf16[64,8,128]{2,1,0:T(8,128)(2,1)}, u32[]{:S(2)}, u32[]{:S(2)}) async-start(bf16[64,8,128]{2,1,0:T(8,128)(2,1)} %bitcast.162), calls=%async_computation.1 | async-start | bytes 262144 | tf_op jit(solution)/shard_map/all_to_all | solution.py:90
  287.3 1.6 fusion.8
  288.9 2.7 convolution_add_fusion.4
  291.6 11.3 %all-to-all-done.1 = bf16[64,8,128]{2,1,0:T(8,128)(2,1)} async-done(((bf16[64,8,128]{2,1,0:T(8,128)(2,1)}), bf16[64,8,128]{2,1,0:T(8,128)(2,1)}, u32[]{:S(2)}, u32[]{:S(2)}) %all-to-all-start.1) | async-done | bytes 131104 | tf_op jit(solution)/shard_map/all_to_all | solution.py:90
  302.9 1.4 convolution_negate_fusion.1
  304.3 1.3 fusion.64
  305.6 0.8 fusion.18
  306.4 0.8 fusion.14
  307.3 0.8 convolution_add_fusion.3
  308.1 0.8 convolution_subtract_fusion.3
  309.0 1.0 multiply_subtract_fusion
  310.0 0.8 fusion.84
  310.8 0.8 fusion.97
  311.6 0.8 convolution_add_fusion.2
  312.5 0.8 convolution_subtract_fusion.2
  313.3 0.5 fusion.36
  313.8 0.5 fusion.5
  314.3 0.7 copy.46
  315.0 5.4 %all-to-all-start.2 = ((bf16[8,64,128]{2,0,1:T(8,128)(2,1)}), bf16[8,64,128]{2,0,1:T(8,128)(2,1)S(1)}, u32[]{:S(2)}, u32[]{:S(2)}) async-start(bf16[8,64,128]{2,0,1:T(8,128)(2,1)} %copy.46), calls=%async_computation.2 | async-start | bytes 262144 | tf_op jit(solution)/shard_map/all_to_all | solution.py:109
  320.5 0.8 fusion.79
  321.3 0.8 fusion.92
  322.1 0.8 convolution_add_fusion
  322.9 0.8 convolution_subtract_fusion
  323.7 0.5 fusion.29
  324.2 0.5 fusion.4
  324.8 0.1 copy.52
  324.9 11.6 %all-to-all-done.2 = bf16[8,64,128]{2,0,1:T(8,128)(2,1)S(1)} async-done(((bf16[8,64,128]{2,0,1:T(8,128)(2,1)}), bf16[8,64,128]{2,0,1:T(8,128)(2,1)S(1)}, u32[]{:S(2)}, u32[]{:S(2)}) %all-to-all-start.2) | async-done | bytes 131104 | tf_op jit(solution)/shard_map/all_to_all | solution.py:109
  336.5 20.0 %all_to_all.93 = bf16[8,64,128]{2,0,1:T(8,128)(2,1)S(1)} all-to-all(bf16[8,64,128]{2,0,1:T(8,128)(2,1)S(1)} %copy.52), channel_id=1, replica_groups=mesh['ctx'=64,'ch'=8] {'ctx'}, dimensions={1} | all-to-all | bytes 262144 | tf_op jit(solution)/shard_map/all_to_all | solution.py:110
  356.5 4.8 %all-to-all-start.5 = ((bf16[128,64,64]{0,2,1:T(8,128)(2,1)}), bf16[128,64,64]{0,2,1:T(8,128)(2,1)S(1)}, u32[]{:S(2)}, u32[]{:S(2)}) async-start(bf16[128,64,64]{0,2,1:T(8,128)(2,1)} %bitcast.33), calls=%async_computation.5 | async-start | bytes 2097152 | tf_op jit(solution)/shard_map/all_to_all | solution.py:116
  361.3 1.0 fusion.44
  362.3 0.8 copy.54
  363.1 0.8 copy.55
  363.8 0.8 copy.56
  364.6 48.2 %all-to-all-done.5 = bf16[128,64,64]{0,2,1:T(8,128)(2,1)S(1)} async-done(((bf16[128,64,64]{0,2,1:T(8,128)(2,1)}), bf16[128,64,64]{0,2,1:T(8,128)(2,1)S(1)}, u32[]{:S(2)}, u32[]{:S(2)}) %all-to-all-start.5) | async-done | bytes 1048608 | tf_op jit(solution)/shard_map/all_to_all | solution.py:116
  412.8 5.8 %fusion.56 = (bf16[64,512]{1,0:T(8,128)(2,1)}, f32[64,512]{1,0:T(8,128)}, f32[64,512]{1,0:T(8,128)}) fusion(bf16[64,512]{1,0:T(8,128)(2,1)} %param.15, f32[64,512]{1,0:T(8,128)} %param.16, f32[64,512]{1,0:T(8,128)} %param.17, bf16[8192,512]{1,0:T(8,128)(2,1)} %all-gather.8.cloned.1.call-done, bf16[128,64,64]{0,2,1:T(8,128)(2,1)S(1)} %all-to-all-done.5), kind=kOutput, calls=%fused_computation.91 | convolution fusion | flops 537427968 | bytes 10092544 | tf_op jit(solution)/shard_map/dot_general | solution.py:117
  (13 shorter events, 0.1 us)
Async XLA Ops:
  7.2 98.3 %all-gather.4.cloned.1.call-start = ((), (), s32[]{:S(2)}) async-start(), calls=%async_computation.6 | async-start | bytes 1179648 | tf_op jit(solution)/shard_map/all_gather | solution.py:77
  8.9 214.6 %all-gather.6.cloned.1.call-start = ((), (), s32[]{:S(2)}) async-start(), calls=%async_computation.7 | async-start | bytes 4259840 | tf_op jit(solution)/shard_map/all_gather | solution.py:84
  9.7 403.1 %all-gather.8.cloned.1.call-start = ((), (), s32[]{:S(2)}) async-start(), calls=%async_computation.8 | async-start | bytes 8519680 | tf_op jit(solution)/shard_map/all_gather | solution.py:119
  229.6 9.7 %copy-start.2 = (bf16[128,512]{0,1:T(8,128)(2,1)}, bf16[128,512]{0,1:T(8,128)(2,1)S(1)}, u32[]{:S(2)}) copy-start(bf16[128,512]{0,1:T(8,128)(2,1)S(1)} %copy.47) | copy-start | bytes 393220
  230.3 22.9 %all-to-all-start.3 = ((bf16[64,8,128]{2,1,0:T(8,128)(2,1)}), bf16[64,8,128]{2,1,0:T(8,128)(2,1)S(1)}, u32[]{:S(2)}, u32[]{:S(2)}) async-start(bf16[64,8,128]{2,1,0:T(8,128)(2,1)} %fusion.58), calls=%async_computation.3 | async-start | bytes 262144 | tf_op jit(solution)/shard_map/all_to_all | solution.py:91
  253.2 21.4 %all-to-all-start = ((bf16[64,8,128]{2,1,0:T(8,128)(2,1)}), bf16[64,8,128]{2,1,0:T(8,128)(2,1)S(1)}, u32[]{:S(2)}, u32[]{:S(2)}) async-start(bf16[64,8,128]{2,1,0:T(8,128)(2,1)} %bitcast.3), calls=%async_computation | async-start | bytes 262144 | tf_op jit(solution)/shard_map/all_to_all | solution.py:92
  282.1 20.8 %all-to-all-start.1 = ((bf16[64,8,128]{2,1,0:T(8,128)(2,1)}), bf16[64,8,128]{2,1,0:T(8,128)(2,1)}, u32[]{:S(2)}, u32[]{:S(2)}) async-start(bf16[64,8,128]{2,1,0:T(8,128)(2,1)} %bitcast.162), calls=%async_computation.1 | async-start | bytes 262144 | tf_op jit(solution)/shard_map/all_to_all | solution.py:90
  302.8 6.1 %copy-start = (f32[8,128,128]{2,1,0:T(8,128)S(1)}, f32[8,128,128]{2,1,0:T(8,128)}, u32[]{:S(2)}) copy-start(f32[8,128,128]{2,1,0:T(8,128)} %convolution_add_fusion.4) | copy-start | bytes 1572868
  302.9 6.1 %copy-start.1 = (f32[8,128,128]{2,1,0:T(8,128)S(1)}, f32[8,128,128]{2,1,0:T(8,128)}, u32[]{:S(2)}) copy-start(f32[8,128,128]{2,1,0:T(8,128)} %fusion.8) | copy-start | bytes 1572868
  312.4 48.9 %copy-start.3 = (bf16[128,512]{0,1:T(8,128)(2,1)S(1)}, bf16[128,512]{0,1:T(8,128)(2,1)}, u32[]{:S(2)}) copy-start(bf16[128,512]{0,1:T(8,128)(2,1)} %copy-done.2) | copy-start | bytes 393220
  315.0 21.5 %all-to-all-start.2 = ((bf16[8,64,128]{2,0,1:T(8,128)(2,1)}), bf16[8,64,128]{2,0,1:T(8,128)(2,1)S(1)}, u32[]{:S(2)}, u32[]{:S(2)}) async-start(bf16[8,64,128]{2,0,1:T(8,128)(2,1)} %copy.46), calls=%async_computation.2 | async-start | bytes 262144 | tf_op jit(solution)/shard_map/all_to_all | solution.py:109
  336.5 20.0 %copy-start.4 = (bf16[8,64,128]{2,0,1:T(8,128)(2,1)}, bf16[8,64,128]{2,0,1:T(8,128)(2,1)S(1)}, u32[]{:S(2)}) copy-start(bf16[8,64,128]{2,0,1:T(8,128)(2,1)S(1)} %all-to-all-done.2) | copy-start | bytes 393220
  356.5 56.3 %all-to-all-start.5 = ((bf16[128,64,64]{0,2,1:T(8,128)(2,1)}), bf16[128,64,64]{0,2,1:T(8,128)(2,1)S(1)}, u32[]{:S(2)}, u32[]{:S(2)}) async-start(bf16[128,64,64]{0,2,1:T(8,128)(2,1)} %bitcast.33), calls=%async_computation.5 | async-start | bytes 2097152 | tf_op jit(solution)/shard_map/all_to_all | solution.py:116
Sparse Core Ops, SparseCore 0:
  11.8 93.6 all-gather.3
  107.6 115.8 all-gather.5
  227.6 136.8 all-gather.7
where the time goes:
time: 427 us; the launch traced here: 425 us
  waiting for transfers between devices  314 us (74%)
  matrix products  36.2 us (8%)
  starting transfers between devices  28.2 us (7%)
  blocking collectives  20 us (5%)
  between operations  14.1 us (3%)
  local copies, waits for them, and re-layouts  10.2 us (2%)
    all_gather x1, waiting for transfers between devices, on_device(): lax.all_gather(out_weight, 'ctx', axis=0, tiled=True)  118 us
    all_gather x1, waiting for transfers between devices, on_device(): grad_full = lax.all_gather(out_grad, 'ch', axis=1, tiled=True)  95.7 us
    all_to_all x1, waiting for transfers between devices, on_device(): lax.all_to_all(grad_full, 'ctx', split_axis=1, concat_axis=0, tiled=True)  48.2 us
    dot_general x30, matrix products, mixing(): jnp.einsum(form, left, table, precision=lax.Precision.HIGHEST, preferred_...  26.4 us
    all_to_all x1, blocking collectives, on_device(): lax.all_to_all(filt_grad_chan, 'ctx', split_axis=1, concat_axis=0, tiled=...  20 us
    all_to_all x1, waiting for transfers between devices, on_device(): lax.all_to_all(filters.T, 'ctx', split_axis=0, concat_axis=1, tiled=True)  15 us
    all_to_all x1, waiting for transfers between devices, on_device(): lax.all_to_all(key_value.T, 'ctx', split_axis=0, concat_axis=1, tiled=True)  13.3 us
    all_to_all x1, waiting for transfers between devices, on_device(): lax.all_to_all(delta_chan, 'ctx', split_axis=1, concat_axis=0, tiled=True)  11.6 us
  transfers between devices with their start and end apart: 8, of which 7 were waited for; matrix products, arithmetic and copies ran while one was open for 9% of the time, Pallas kernels for 0%

commit v1 on v0

v1 whole, which is shorter than its diff:
```python
import math

import jax
import jax.numpy as jnp
import numpy as np
from jax import lax
from jax.experimental import pallas as pl
from jax.experimental.pallas import tpu as pltpu
from jax.sharding import PartitionSpec as P

BETA_ONE = 0.9
BETA_TWO = 0.95
STEP_RATE = 0.003
DECAY = 0.1
ADAM_STABILIZER = 1e-08

MESH = pl.DeviceIdType.MESH
F32 = jnp.float32
BF16 = jnp.bfloat16
HALF = 72


def halves(table):
    high = table.astype(np.float32).astype(BF16)
    low = (table.astype(np.float32) - high.astype(np.float32)).astype(BF16)
    return high, low


def dft_tables():
    k = np.arange(HALF)[:, None]
    j = np.arange(64)[None, :]
    outer = 2.0 * math.pi * ((k * j) % 128) / 128
    first = np.concatenate([np.cos(outer), -np.sin(outer)], axis=0)
    first = np.concatenate(halves(first), axis=0)
    swapped = np.concatenate([first[:, 0::2], first[:, 1::2]], axis=1)
    m = np.arange(128)[None, :]
    turn = 2.0 * math.pi * (k * m) / 16384
    twist = np.stack([np.cos(turn), np.sin(turn)]).astype(np.float32)
    inner = 2.0 * math.pi * ((np.arange(128)[:, None] * m) % 128) / 128
    c, s = np.cos(inner), np.sin(inner)
    forth = np.stack(halves(np.block([[c, -s], [s, c]])))
    back = np.stack(halves(np.block([[c, s], [-s, c]])))
    weight = np.where((k == 0) | (k == 64), 1.0, np.where(k < 64, 2.0, 0.0)) / 16384
    last = np.concatenate([weight * np.cos(outer), -weight * np.sin(outer)], axis=0).T
    last = np.stack(halves(last))
    return first, swapped, twist, forth, back, last


def three(left, high, low):
    left_high = left.astype(BF16)
    left_low = (left - left_high.astype(F32)).astype(BF16)
    return (
        jnp.dot(left_high, high, preferred_element_type=F32)
        + jnp.dot(left_low, high, preferred_element_type=F32)
        + jnp.dot(left_high, low, preferred_element_type=F32)
    )


def kernel(
    q_ref, k_ref, v_ref, z_ref, h_ref, g_ref, w_ref,
    first_ref, swapped_ref, twist_ref, forth_ref, back_ref, last_ref,
    qg_ref, vd_ref, fg_ref, wg_ref,
    ga, gp, wa, pa, skf, rkf, s1, r1, acc1, sc, rc, acc2, sa, ra, sb, rb, sd, rd,
    sg, rg, sf, rf, fs, dd, aa, spec, xx,
    grad_s, grad_r, gp_s, gp_r, w_s, w_r, p_s, p_r, kf_s, kf_r, one_s, one_r, two_s, two_r,
    g_s, g_r, f_s, f_r,
):
    ctx, ch = lax.axis_index("ctx"), lax.axis_index("ch")
    zl, y, core = ctx // 8, (ctx // 2) % 4, ctx % 2
    chip = ctx // 2
    x, zh = ch % 4, ch // 4
    sib = (chip * 2 + 1 - core, ch)
    far = (ctx, lax.rem(ch + 4, 8))
    z1 = zl + 1 - 2 * (zl % 2)
    z2 = zl + 2 - 4 * ((zl // 2) % 2)
    z4 = lax.rem(zl + 4, 8)

    def place(zz):
        return (zz * 8 + y * 2 + core, ch)

    def remote(src, dst, send, recv, device):
        return pltpu.make_async_remote_copy(
            src_ref=src, dst_ref=dst, send_sem=send, recv_sem=recv, device_id=device, device_id_type=MESH
        )

    def drain(ref, sem):
        pltpu.make_async_copy(ref, ref, sem).wait()

    entry = pltpu.get_barrier_semaphore()

    def greet(d, carry):
        pl.semaphore_signal(entry, 1, device_id=(lax.rem(ctx + d, 64), ch), device_id_type=MESH)
        return carry

    lax.fori_loop(1, 64, greet, 0)

    def near(d):
        x_to, y_to = lax.rem(x + d // 4, 4), lax.rem(y + d % 4, 4)
        return x_to, y_to, (zl * 8 + y_to * 2 + core, zh * 4 + x_to)

    def greet_near(d, carry):
        pl.semaphore_signal(entry, 1, device_id=near(d)[2], device_id_type=MESH)
        return carry

    lax.fori_loop(4, 16, greet_near, 0)
    pl.semaphore_signal(entry, 1, device_id=far, device_id_type=MESH)

    pa[y] = (q_ref[...].astype(F32) * z_ref[...].astype(F32)).astype(BF16)
    wa[zl, core] = w_ref[...]

    def stage_pair(t, carry):
        cols = pl.ds(pl.multiple_of(t * 128, 128), 128)
        kv = (k_ref[:, cols].astype(F32) * v_ref[:, cols].astype(F32)).T.reshape(16, 8, 128)
        filt = h_ref[:, cols].astype(F32).T.reshape(16, 8, 128)
        skf[pl.ds(t * 16, 16)] = jnp.concatenate([kv, filt], axis=1).astype(BF16)
        return carry

    lax.fori_loop(0, 4, stage_pair, 0)
    rkf[ctx] = skf[ctx]
    pl.semaphore_wait(entry, 76)

    far_copy = remote(g_ref, gp, gp_s, gp_r, far)
    far_copy.start()

    def send_w(block, device, step):
        return remote(wa.at[block, core], wa.at[block, core], w_s.at[step], w_r.at[step], device)

    send_w(zl, place(z4), 0).start()
    send_w(zl, sib, 3).start()

    def spread(src, row, half):
        def body(d, carry):
            x_to, y_to, device = near(d)
            cols = pl.ds(pl.multiple_of(y_to * 128, 128), 128)
            remote(src.at[:, cols], ga.at[row, x * 4 + y], grad_s.at[half], grad_r.at[half], device).start()
            return carry

        lax.fori_loop(1, 16, body, 0)
        ga[row, x * 4 + y] = src[:, pl.ds(pl.multiple_of(y * 128, 128), 128)]

    spread(g_ref, zh, 0)
    for d in range(1, 4):
        y_to = lax.rem(y + d, 4)
        remote(pa.at[y], pa.at[y], p_s, p_r, (zl * 8 + y_to * 2 + core, ch)).start()

    drain(wa.at[0, 0], w_r.at[0])
    send_w(zl, place(z2), 1).start()
    send_w(z4, place(z2), 1).start()
    send_w(z4, sib, 3).start()
    drain(wa.at[pl.ds(0, 2), 0], w_r.at[1])
    z24 = lax.rem(z2 + 4, 8)
    for block in (zl, z4, z2, z24):
        send_w(block, place(z1), 2).start()
    send_w(z2, sib, 3).start()
    send_w(z24, sib, 3).start()

    far_copy.wait_recv()
    spread(gp, 1 - zh, 1)

    def send_pair(d, carry):
        to = lax.rem(ctx + d, 64)
        remote(skf.at[to], rkf.at[ctx], kf_s, kf_r, (to, ch)).start()
        return carry

    lax.fori_loop(1, 64, send_pair, 0)

    drain(wa.at[pl.ds(0, 4), 0], w_r.at[2])
    for block in (z1, lax.rem(z1 + 4, 8), z1 + 2 - 4 * ((z1 // 2) % 2), lax.rem(z1 + 6 - 4 * ((z1 // 2) % 2), 8)):
        send_w(block, sib, 3).start()
    drain(wa.at[:, 0], w_r.at[3])
    drain(ga.at[0, pl.ds(0, 15)], grad_r.at[0])

    acc1[...] = jnp.zeros_like(acc1)

    def multiply(row):
        def body(t, carry):
            left = ga[row, pl.ds(t * 4, 4)].reshape(512, 128)
            right = wa[row * 4 + t].reshape(128, 512)
            acc1[...] += jnp.dot(left, right, preferred_element_type=F32)
            return carry

        lax.fori_loop(0, 4, body, 0)

    multiply(zh)
    drain(ga.at[0, pl.ds(0, 15)], grad_r.at[1])
    multiply(1 - zh)
    for d in range(1, 4):
        y_to = lax.rem(y + d, 4)
        s1[d - 1] = acc1[pl.ds(pl.multiple_of(y_to * 128, 128), 128), :].astype(BF16)
        remote(s1.at[d - 1], r1.at[d - 1], one_s, one_r, (zl * 8 + y_to * 2 + core, ch)).start()

    drain(pa.at[pl.ds(0, 3)], p_r)
    first_core = core == 0

    def partial_rows(t, carry):
        left = ga[t // 4, pl.ds((t % 4) * 4, 4)].reshape(512, 128)
        part = lax.dot_general(
            left, pa[...].reshape(512, 512), (((0,), (0,)), ((), ())), preferred_element_type=F32
        )
        top, low = part[:64], part[64:]
        acc2[t] = jnp.where(first_core, top, low)
        sc[t] = jnp.where(first_core, low, top).astype(BF16)
        return carry

    lax.fori_loop(0, 8, partial_rows, 0)
    core_copy = remote(sc, rc, two_s.at[0], two_r.at[0], sib)
    core_copy.start()

    drain(r1, one_r)
    delta = acc1[pl.ds(pl.multiple_of(y * 128, 128), 128), :]
    for d in range(3):
        delta = delta + r1[d].astype(F32)
    qg_ref[...] = (delta * z_ref[...].astype(F32)).astype(BF16)
    conv = (delta * q_ref[...].astype(F32)).astype(BF16).astype(F32)
    sg[...] = conv.T.reshape(32, 16, 128).astype(BF16)
    rg[core, chip] = sg[chip]

    def send_conv(d, carry):
        to = lax.rem(chip + d, 32)
        remote(sg.at[to], rg.at[core, chip], g_s.at[0], g_r.at[0], (to * 2 + core, ch)).start()
        return carry

    lax.fori_loop(1, 32, send_conv, 0)

    core_copy.wait_recv()
    bit0, bit1, bit2 = zl % 2, (zl // 2) % 2, zl // 4
    for i in range(4):
        give, keep = 2 * i + 1 - bit0, 2 * i + bit0
        sa[i] = (acc2[give] + rc[give].astype(F32)).astype(BF16)
        acc2[keep] = acc2[keep] + rc[keep].astype(F32)
    a_copy = remote(sa, ra, two_s.at[1], two_r.at[1], place(z1))
    a_copy.start()

    twist_cos, twist_sin = twist_ref[0], twist_ref[1]

    def spectrum(base, table, slot):
        for c in range(8):
            dd[:, c * 128 : (c + 1) * 128] = fs[pl.ds(base + c, 64, stride=16), :].astype(BF16)
        both = jnp.dot(table[...], dd[...], preferred_element_type=F32)
        both = both[: 2 * HALF] + both[2 * HALF :]
        for c in range(8):
            real = both[:HALF, c * 128 : (c + 1) * 128]
            imag = both[HALF:, c * 128 : (c + 1) * 128]
            aa[c * HALF : (c + 1) * HALF, :128] = real * twist_cos + imag * twist_sin
            aa[c * HALF : (c + 1) * HALF, 128:] = imag * twist_cos - real * twist_sin
        spec[slot] = three(aa[...], forth_ref[0], forth_ref[1])

    drain(rkf.at[pl.ds(0, 63)], kf_r)
    fs[...] = rkf[...].astype(F32).reshape(1024, 128)
    spectrum(0, first_ref, 0)
    spectrum(8, first_ref, 1)

    a_copy.wait_recv()
    for i in range(2):
        give, keep = 2 * i + 1 - bit1, 2 * i + bit1
        sb[i] = (acc2[2 * give + bit0] + ra[give].astype(F32)).astype(BF16)
        acc2[2 * keep + bit0] = acc2[2 * keep + bit0] + ra[keep].astype(F32)
    b_copy = remote(sb, rb, two_s.at[2], two_r.at[2], place(z2))
    b_copy.start()

    drain(rg.at[0, pl.ds(0, 31)], g_r.at[0])
    g_copy = remote(rg.at[core], rg.at[core], g_s.at[1], g_r.at[1], sib)
    g_copy.start()

    b_copy.wait_recv()
    give, keep = 1 - bit2, bit2
    sd[...] = (acc2[4 * give + 2 * bit1 + bit0] + rb[give].astype(F32)).astype(BF16)
    d_copy = remote(sd, rd, two_s.at[3], two_r.at[3], place(z4))
    d_copy.start()
    mine = acc2[4 * keep + 2 * bit1 + bit0] + rb[keep].astype(F32)
    wg_ref[...] = mine

    g_copy.wait_recv()
    fs[...] = rg[...].astype(F32).reshape(1024, 128)
    spectrum(core * 8, swapped_ref, 2)

    for slot, base in ((1, 0), (0, 8)):
        other_real, other_imag = spec[slot, :, :128], spec[slot, :, 128:]
        grad_real, grad_imag = spec[2, :, :128], spec[2, :, 128:]
        aa[:, :128] = other_real * grad_real + other_imag * grad_imag
        aa[:, 128:] = other_real * grad_imag - other_imag * grad_real
        turned = three(aa[...], back_ref[0], back_ref[1])
        for c in range(8):
            real = turned[c * HALF : (c + 1) * HALF, :128]
            imag = turned[c * HALF : (c + 1) * HALF, 128:]
            xx[:HALF, c * 128 : (c + 1) * 128] = real * twist_cos - imag * twist_sin
            xx[HALF:, c * 128 : (c + 1) * 128] = real * twist_sin + imag * twist_cos
        right = xx[...]
        right_high = right.astype(BF16)
        right_low = (right - right_high.astype(F32)).astype(BF16)
        signal = (
            jnp.dot(last_ref[0], right_high, preferred_element_type=F32)
            + jnp.dot(last_ref[0], right_low, preferred_element_type=F32)
            + jnp.dot(last_ref[1], right_high, preferred_element_type=F32)
        )
        for c in range(8):
            fs[pl.ds(base + c, 64, stride=16), :] = signal[:, c * 128 : (c + 1) * 128]
    sf[...] = fs[...].astype(BF16).reshape(64, 16, 128)
    rf[ctx] = sf[ctx]

    def send_back(d, carry):
        to = lax.rem(ctx + d, 64)
        remote(sf.at[to], rf.at[ctx], f_s, f_r, (to, ch)).start()
        return carry

    lax.fori_loop(1, 64, send_back, 0)

    d_copy.wait_recv()
    wg_ref[...] = wg_ref[...] + rd[...].astype(F32)

    far_copy.wait_send()
    drain(wa.at[0, 0], w_s.at[0])
    drain(wa.at[pl.ds(0, 2), 0], w_s.at[1])
    drain(wa.at[pl.ds(0, 4), 0], w_s.at[2])
    drain(wa.at[:, 0], w_s.at[3])
    drain(ga.at[0, pl.ds(0, 15)], grad_s.at[0])
    drain(ga.at[0, pl.ds(0, 15)], grad_s.at[1])
    drain(pa.at[pl.ds(0, 3)], p_s)
    drain(skf.at[pl.ds(0, 63)], kf_s)
    drain(s1, one_s)
    core_copy.wait_send()
    a_copy.wait_send()
    b_copy.wait_send()
    d_copy.wait_send()
    drain(sg.at[pl.ds(0, 31)], g_s.at[0])
    g_copy.wait_send()

    drain(rf.at[pl.ds(0, 63)], f_r)
    for t in range(4):
        back = rf[t * 16 : (t + 1) * 16].astype(F32)
        vd_ref[:, t * 128 : (t + 1) * 128] = back[:, :8].reshape(128, 128).T.astype(BF16)
        fg_ref[:, t * 128 : (t + 1) * 128] = back[:, 8:].reshape(128, 128).T.astype(BF16)
    drain(sf.at[pl.ds(0, 63)], f_s)


def on_device(
    queries, keys, values, conv_out, filters, out_grad, out_weight, moment_one, moment_two
):
    tables = [jnp.asarray(t) for t in dft_tables()]
    vmem = pl.BlockSpec(memory_space=pltpu.VMEM)
    dma = pltpu.SemaphoreType.DMA

    def half(*shape):
        return pltpu.VMEM(shape, BF16)

    def full(*shape):
        return pltpu.VMEM(shape, F32)

    query_grad, value_delta, filter_grad, weight_grad = pl.pallas_call(
        kernel,
        out_shape=(
            jax.ShapeDtypeStruct((128, 512), BF16),
            jax.ShapeDtypeStruct((128, 512), BF16),
            jax.ShapeDtypeStruct((128, 512), BF16),
            jax.ShapeDtypeStruct((64, 512), F32),
        ),
        in_specs=[vmem] * 13,
        out_specs=(vmem,) * 4,
        scratch_shapes=[
            half(2, 16, 128, 128),
            half(128, 512),
            half(8, 2, 64, 512),
            half(4, 128, 512),
            half(64, 16, 128),
            half(64, 16, 128),
            half(3, 128, 512),
            half(3, 128, 512),
            full(512, 512),
            half(8, 64, 512),
            half(8, 64, 512),
            full(8, 64, 512),
            half(4, 64, 512),
            half(4, 64, 512),
            half(2, 64, 512),
            half(2, 64, 512),
            half(64, 512),
            half(64, 512),
            half(32, 16, 128),
            half(2, 32, 16, 128),
            half(64, 16, 128),
            half(64, 16, 128),
            full(1024, 128),
            half(64, 1024),
            full(8 * HALF, 256),
            full(3, 8 * HALF, 256),
            full(2 * HALF, 1024),
            dma((2,)), dma((2,)),
            dma, dma,
            dma((4,)), dma((4,)),
            dma, dma,
            dma, dma,
            dma, dma,
            dma((4,)), dma((4,)),
            dma((2,)), dma((2,)),
            dma, dma,
        ],
        compiler_params=pltpu.CompilerParams(
            collective_id=1, has_side_effects=True, vmem_limit_bytes=40 * 2**20
        ),
    )(queries, keys, values, conv_out, filters, out_grad, out_weight, *tables)

    delta = value_delta.astype(F32)
    key_grad = (delta * values.astype(F32)).astype(BF16)
    value_grad = (delta * keys.astype(F32)).astype(BF16)
    new_moment_one = BETA_ONE * moment_one + (1.0 - BETA_ONE) * weight_grad
    new_moment_two = BETA_TWO * moment_two + (1.0 - BETA_TWO) * weight_grad * weight_grad
    corr_one = 1.0 - BETA_ONE**10
    corr_two = 1.0 - BETA_TWO**10
    weight_float = out_weight.astype(F32)
    update = new_moment_one / corr_one / (jnp.sqrt(new_moment_two / corr_two) + ADAM_STABILIZER)
    new_weight = (weight_float - STEP_RATE * (update + DECAY * weight_float)).astype(BF16)
    return (
        query_grad,
        key_grad,
        value_grad,
        filter_grad,
        new_weight,
        new_moment_one,
        new_moment_two,
    )


def solution(mesh):
    spec = P("ctx", "ch")
    return jax.shard_map(
        on_device, mesh=mesh, in_specs=(spec,) * 9, out_specs=(spec,) * 7, check_vma=False
    )
```

time: 427 us -> 118 us (0.28)
  waiting for transfers between devices: 314 us -> 0 us
  Pallas kernels: 0 us -> 102 us
  matrix products: 36.2 us -> 0 us
  starting transfers between devices: 28.2 us -> 0 us
  blocking collectives: 20 us -> 0 us
  between operations: 14.1 us -> 0.68 us
    all_gather x3 -> x0, waiting for transfers between devices: 214 us -> none  [the longest x1 118 us: on_device(): lax.all_gather(out_weight, 'ctx', axis=0, tiled=True)]
    pallas_call x0 -> x1, Pallas kernels: none -> 102 us  [on_device(): pl.pallas_call(kernel, out_shape=(jax.ShapeDtypeStruct((128, 512), BF16),...]
    all_to_all x5 -> x0, waiting for transfers between devices: 99.5 us -> none  [the longest x1 48.2 us: on_device(): lax.all_to_all(grad_full, 'ctx', split_axis=1, concat_axis=0, tiled=True)]
    dot_general x32 -> x0, matrix products: 36.2 us -> none  [the longest x30 26.4 us: mixing(): jnp.einsum(form, left, table, precision=lax.Precision.HIGHEST, preferred_...]
    all_to_all x5 -> x0, starting transfers between devices: 28.1 us -> none  [the longest x1 7.35 us: on_device(): lax.all_to_all(key_value.T, 'ctx', split_axis=0, concat_axis=1, tiled=True)]
    all_to_all x1 -> x0, blocking collectives: 20 us -> none  [on_device(): lax.all_to_all(filt_grad_chan, 'ctx', split_axis=1, concat_axis=0, tiled=...]
    unnamed x17 -> x32, local copies, waits for them, and re-layouts: 7.71 us -> 13.2 us
  transfers between devices with their start and end apart: 8 -> 0, of which waited for: 7 -> 0; matrix products, arithmetic and copies ran while one was open for 9% -> 0% of each run, Pallas kernels for 0% -> 0%
where the time goes in v1:
time: 118 us; the launch traced here: 117 us
  Pallas kernels  102 us (86%)
  local copies, waits for them, and re-layouts  13.2 us (11%)
  other arithmetic  1.53 us (1%)
    pallas_call x1, Pallas kernels, on_device(): pl.pallas_call(kernel, out_shape=(jax.ShapeDtypeStruct((128, 512), BF16),...  102 us
    unnamed x32, local copies, waits for them, and re-layouts  13.2 us

profile of v1, /device:TPU:7, one launch (start us, length us, event | category | flops | bytes accessed | tf_op | source)
XLA Modules:
  0.0 117.2 jit_solution(6645282789983150783)
XLA Ops:
  0.6 0.0 copy-start
  0.6 0.9 copy-done
  1.5 0.0 copy-start.1
  1.5 0.9 copy-done.1
  2.4 0.0 copy-start.2
  2.4 0.9 copy-done.2
  3.4 0.0 copy-start.3
  3.4 0.9 copy-done.3
  4.3 0.0 copy-start.4
  4.3 0.8 copy-done.4
  5.2 0.0 copy-start.5
  5.2 0.9 copy-done.5
  6.1 0.0 copy-start.6
  6.1 0.9 copy-done.6
  7.0 0.0 copy-start.7
  7.0 0.9 copy-done.7
  7.9 0.0 copy-start.8
  7.9 0.9 copy-done.8
  8.8 0.0 copy-start.9
  8.8 0.9 copy-done.9
  9.7 0.0 copy-start.10
  9.7 0.9 copy-done.10
  10.6 0.0 copy-start.11
  10.6 0.9 copy-done.11
  11.5 0.0 copy-start.12
  11.5 0.8 copy-done.12
  12.3 101.8 %shard_map.198 = (bf16[128,512]{1,0:T(8,128)(2,1)S(1)}, bf16[128,512]{1,0:T(8,128)(2,1)S(1)}, bf16[128,512]{1,0:T(8,128)(2,1)S(1)}, f32[64,512]{1,0:T(8,128)S(1)}) custom-call(bf16[128,512]{1,0:T(8,128)(2,1)S(1)} %copy-done.5, bf16[128,512]{1,0:T(8,128)(2,1)S(1)} %copy-done, bf16[128,512]{1,0:T(8,128)(2,1)S(1)} %copy-done.1, bf16[128,512]{1,0:T(8,128)(2,1)S(1)} %copy-done.6, ...), custom_call_target="tpu_custom_call" | custom-call | tf_op jit(solution)/shard_map/pallas_call | solution.py:349
  114.1 0.0 copy-start.13
  114.1 0.0 copy-start.14
  114.1 0.8 fusion.1
  114.9 0.1 copy-done.13
  115.0 0.1 copy-done.14
  115.2 0.8 fusion.4
  115.9 0.7 copy.24
  116.6 0.7 copy.25
Async XLA Ops:
  0.6 0.9 copy-start
  1.5 0.9 copy-start.1
  2.4 0.9 copy-start.2
  3.4 0.9 copy-start.3
  4.3 0.8 copy-start.4
  5.2 0.9 copy-start.5
  6.1 0.9 copy-start.6
  7.0 0.9 copy-start.7
  7.9 0.9 copy-start.8
  8.8 0.9 copy-start.9
  9.7 0.9 copy-start.10
  10.6 0.9 copy-start.11
  11.5 0.8 copy-start.12
  114.1 0.9 copy-start.13
  114.1 1.0 copy-start.14

commit v2 on v1

--- a/solution.py
+++ b/solution.py
@@ -57,13 +57,15 @@
 
 
 def kernel(
-    q_ref, k_ref, v_ref, z_ref, h_ref, g_ref, w_ref,
+    q_in, k_in, v_in, z_in, h_in, g_in, w_in,
+    first_in, swapped_in, twist_in, forth_in, back_in, last_in,
+    qg_ref, vd_ref, fg_ref, wg_ref,
+    q_ref, k_ref, v_ref, z_ref, h_ref, g_ref,
     first_ref, swapped_ref, twist_ref, forth_ref, back_ref, last_ref,
-    qg_ref, vd_ref, fg_ref, wg_ref,
     ga, gp, wa, pa, skf, rkf, s1, r1, acc1, sc, rc, acc2, sa, ra, sb, rb, sd, rd,
     sg, rg, sf, rf, fs, dd, aa, spec, xx,
     grad_s, grad_r, gp_s, gp_r, w_s, w_r, p_s, p_r, kf_s, kf_r, one_s, one_r, two_s, two_r,
-    g_s, g_r, f_s, f_r,
+    g_s, g_r, f_s, f_r, load,
 ):
     ctx, ch = lax.axis_index("ctx"), lax.axis_index("ch")
     zl, y, core = ctx // 8, (ctx // 2) % 4, ctx % 2
@@ -86,6 +88,15 @@
     def drain(ref, sem):
         pltpu.make_async_copy(ref, ref, sem).wait()
 
+    owed = {}
+
+    def owe(name, ref, sem):
+        owed[name] = lambda: drain(ref, sem)
+
+    def settle(*names):
+        for name in names or list(owed):
+            owed.pop(name)()
+
     entry = pltpu.get_barrier_semaphore()
 
     def greet(d, carry):
@@ -105,8 +116,17 @@
     lax.fori_loop(4, 16, greet_near, 0)
     pl.semaphore_signal(entry, 1, device_id=far, device_id_type=MESH)
 
+    pairs = (
+        (g_in, g_ref), (w_in, wa.at[zl, core]), (q_in, q_ref), (z_in, z_ref), (k_in, k_ref), (v_in, v_ref), (h_in, h_ref),
+        (first_in, first_ref), (swapped_in, swapped_ref), (twist_in, twist_ref), (forth_in, forth_ref),
+        (back_in, back_ref), (last_in, last_ref),
+    )
+    loads = [pltpu.make_async_copy(src, dst, load.at[i]) for i, (src, dst) in enumerate(pairs)]
+    for copy in loads:
+        copy.start()
+    for copy in loads[:7]:
+        copy.wait()
     pa[y] = (q_ref[...].astype(F32) * z_ref[...].astype(F32)).astype(BF16)
-    wa[zl, core] = w_ref[...]
 
     def stage_pair(t, carry):
         cols = pl.ds(pl.multiple_of(t * 128, 128), 128)
@@ -121,6 +141,13 @@
 
     far_copy = remote(g_ref, gp, gp_s, gp_r, far)
     far_copy.start()
+    owed["far_s"] = far_copy.wait_send
+    owed["far_r"] = far_copy.wait_recv
+    owe("w_s0", wa.at[0, 0], w_s.at[0])
+    owe("w_s1", wa.at[pl.ds(0, 2), 0], w_s.at[1])
+    owe("w_s2", wa.at[pl.ds(0, 4), 0], w_s.at[2])
+    owe("w_s3", wa.at[:, 0], w_s.at[3])
+    owe("w_r3", wa.at[:, 0], w_r.at[3])
 
     def send_w(block, device, step):
         return remote(wa.at[block, core], wa.at[block, core], w_s.at[step], w_r.at[step], device)
@@ -136,9 +163,13 @@
             return carry
 
         lax.fori_loop(1, 16, body, 0)
+        owe(f"grad_s{half}", ga.at[0, pl.ds(0, 15)], grad_s.at[half])
+        owe(f"grad_r{half}", ga.at[0, pl.ds(0, 15)], grad_r.at[half])
         ga[row, x * 4 + y] = src[:, pl.ds(pl.multiple_of(y * 128, 128), 128)]
 
     spread(g_ref, zh, 0)
+    owe("p_s", pa.at[pl.ds(0, 3)], p_s)
+    owe("p_r", pa.at[pl.ds(0, 3)], p_r)
     for d in range(1, 4):
         y_to = lax.rem(y + d, 4)
         remote(pa.at[y], pa.at[y], p_s, p_r, (zl * 8 + y_to * 2 + core, ch)).start()
@@ -154,7 +185,7 @@
     send_w(z2, sib, 3).start()
     send_w(z24, sib, 3).start()
 
-    far_copy.wait_recv()
+    settle("far_r")
     spread(gp, 1 - zh, 1)
 
     def send_pair(d, carry):
@@ -163,12 +194,14 @@
         return carry
 
     lax.fori_loop(1, 64, send_pair, 0)
+    owe("kf_s", skf.at[pl.ds(0, 63)], kf_s)
+    owe("kf_r", rkf.at[pl.ds(0, 63)], kf_r)
 
     drain(wa.at[pl.ds(0, 4), 0], w_r.at[2])
     for block in (z1, lax.rem(z1 + 4, 8), z1 + 2 - 4 * ((z1 // 2) % 2), lax.rem(z1 + 6 - 4 * ((z1 // 2) % 2), 8)):
         send_w(block, sib, 3).start()
-    drain(wa.at[:, 0], w_r.at[3])
-    drain(ga.at[0, pl.ds(0, 15)], grad_r.at[0])
+    settle("w_r3")
+    settle("grad_r0")
 
     acc1[...] = jnp.zeros_like(acc1)
 
@@ -182,14 +215,16 @@
         lax.fori_loop(0, 4, body, 0)
 
     multiply(zh)
-    drain(ga.at[0, pl.ds(0, 15)], grad_r.at[1])
+    settle("grad_r1")
     multiply(1 - zh)
+    owe("one_s", s1, one_s)
+    owe("one_r", r1, one_r)
     for d in range(1, 4):
         y_to = lax.rem(y + d, 4)
         s1[d - 1] = acc1[pl.ds(pl.multiple_of(y_to * 128, 128), 128), :].astype(BF16)
         remote(s1.at[d - 1], r1.at[d - 1], one_s, one_r, (zl * 8 + y_to * 2 + core, ch)).start()
 
-    drain(pa.at[pl.ds(0, 3)], p_r)
+    settle("p_r")
     first_core = core == 0
 
     def partial_rows(t, carry):
@@ -205,8 +240,9 @@
     lax.fori_loop(0, 8, partial_rows, 0)
     core_copy = remote(sc, rc, two_s.at[0], two_r.at[0], sib)
     core_copy.start()
-
-    drain(r1, one_r)
+    owed["core_s"], owed["core_r"] = core_copy.wait_send, core_copy.wait_recv
+
+    settle("one_r")
     delta = acc1[pl.ds(pl.multiple_of(y * 128, 128), 128), :]
     for d in range(3):
         delta = delta + r1[d].astype(F32)
@@ -221,8 +257,10 @@
         return carry
 
     lax.fori_loop(1, 32, send_conv, 0)
-
-    core_copy.wait_recv()
+    owe("g_s", sg.at[pl.ds(0, 31)], g_s.at[0])
+    owe("g_r", rg.at[0, pl.ds(0, 31)], g_r.at[0])
+
+    settle("core_r")
     bit0, bit1, bit2 = zl % 2, (zl // 2) % 2, zl // 4
     for i in range(4):
         give, keep = 2 * i + 1 - bit0, 2 * i + bit0
@@ -230,7 +268,10 @@
         acc2[keep] = acc2[keep] + rc[keep].astype(F32)
     a_copy = remote(sa, ra, two_s.at[1], two_r.at[1], place(z1))
     a_copy.start()
-
+    owed["a_s"], owed["a_r"] = a_copy.wait_send, a_copy.wait_recv
+
+    for copy in loads[7:]:
+        copy.wait()
     twist_cos, twist_sin = twist_ref[0], twist_ref[1]
 
     def spectrum(base, table, slot):
@@ -245,32 +286,35 @@
             aa[c * HALF : (c + 1) * HALF, 128:] = imag * twist_cos - real * twist_sin
         spec[slot] = three(aa[...], forth_ref[0], forth_ref[1])
 
-    drain(rkf.at[pl.ds(0, 63)], kf_r)
+    settle("kf_r")
     fs[...] = rkf[...].astype(F32).reshape(1024, 128)
     spectrum(0, first_ref, 0)
     spectrum(8, first_ref, 1)
 
-    a_copy.wait_recv()
+    settle("a_r")
     for i in range(2):
         give, keep = 2 * i + 1 - bit1, 2 * i + bit1
         sb[i] = (acc2[2 * give + bit0] + ra[give].astype(F32)).astype(BF16)
         acc2[2 * keep + bit0] = acc2[2 * keep + bit0] + ra[keep].astype(F32)
     b_copy = remote(sb, rb, two_s.at[2], two_r.at[2], place(z2))
     b_copy.start()
-
-    drain(rg.at[0, pl.ds(0, 31)], g_r.at[0])
+    owed["b_s"], owed["b_r"] = b_copy.wait_send, b_copy.wait_recv
+
+    settle("g_r")
     g_copy = remote(rg.at[core], rg.at[core], g_s.at[1], g_r.at[1], sib)
     g_copy.start()
-
-    b_copy.wait_recv()
+    owed["gs_s"], owed["gs_r"] = g_copy.wait_send, g_copy.wait_recv
+
+    settle("b_r")
     give, keep = 1 - bit2, bit2
     sd[...] = (acc2[4 * give + 2 * bit1 + bit0] + rb[give].astype(F32)).astype(BF16)
     d_copy = remote(sd, rd, two_s.at[3], two_r.at[3], place(z4))
     d_copy.start()
+    owed["d_s"], owed["d_r"] = d_copy.wait_send, d_copy.wait_recv
     mine = acc2[4 * keep + 2 * bit1 + bit0] + rb[keep].astype(F32)
     wg_ref[...] = mine
 
-    g_copy.wait_recv()
+    settle("gs_r")
     fs[...] = rg[...].astype(F32).reshape(1024, 128)
     spectrum(core * 8, swapped_ref, 2)
 
@@ -304,33 +348,18 @@
         return carry
 
     lax.fori_loop(1, 64, send_back, 0)
-
-    d_copy.wait_recv()
+    owe("f_s", sf.at[pl.ds(0, 63)], f_s)
+    owe("f_r", rf.at[pl.ds(0, 63)], f_r)
+
+    settle("d_r")
     wg_ref[...] = wg_ref[...] + rd[...].astype(F32)
 
-    far_copy.wait_send()
-    drain(wa.at[0, 0], w_s.at[0])
-    drain(wa.at[pl.ds(0, 2), 0], w_s.at[1])
-    drain(wa.at[pl.ds(0, 4), 0], w_s.at[2])
-    drain(wa.at[:, 0], w_s.at[3])
-    drain(ga.at[0, pl.ds(0, 15)], grad_s.at[0])
-    drain(ga.at[0, pl.ds(0, 15)], grad_s.at[1])
-    drain(pa.at[pl.ds(0, 3)], p_s)
-    drain(skf.at[pl.ds(0, 63)], kf_s)
-    drain(s1, one_s)
-    core_copy.wait_send()
-    a_copy.wait_send()
-    b_copy.wait_send()
-    d_copy.wait_send()
-    drain(sg.at[pl.ds(0, 31)], g_s.at[0])
-    g_copy.wait_send()
-
-    drain(rf.at[pl.ds(0, 63)], f_r)
+    settle("f_r")
     for t in range(4):
         back = rf[t * 16 : (t + 1) * 16].astype(F32)
         vd_ref[:, t * 128 : (t + 1) * 128] = back[:, :8].reshape(128, 128).T.astype(BF16)
         fg_ref[:, t * 128 : (t + 1) * 128] = back[:, 8:].reshape(128, 128).T.astype(BF16)
-    drain(sf.at[pl.ds(0, 63)], f_s)
+    settle()
 
 
 def on_device(
@@ -354,9 +383,11 @@
             jax.ShapeDtypeStruct((128, 512), BF16),
             jax.ShapeDtypeStruct((64, 512), F32),
         ),
-        in_specs=[vmem] * 13,
+        in_specs=[pl.BlockSpec(memory_space=pltpu.HBM)] * 13,
         out_specs=(vmem,) * 4,
         scratch_shapes=[
+            *[half(128, 512)] * 6,
+            *[pltpu.VMEM(t.shape, t.dtype) for t in tables],
             half(2, 16, 128, 128),
             half(128, 512),
             half(8, 2, 64, 512),
@@ -393,9 +424,10 @@
             dma((4,)), dma((4,)),
             dma((2,)), dma((2,)),
             dma, dma,
+            dma((13,)),
         ],
         compiler_params=pltpu.CompilerParams(
-            collective_id=1, has_side_effects=True, vmem_limit_bytes=40 * 2**20
+            collective_id=1, has_side_effects=True, vmem_limit_bytes=60 * 2**20
         ),
     )(queries, keys, values, conv_out, filters, out_grad, out_weight, *tables)
 

time: 118 us -> 109 us (0.924)
  local copies, waits for them, and re-layouts: 13.2 us -> 1.78 us
  Pallas kernels: 102 us -> 104 us
    unnamed x32 -> x18, local copies, waits for them, and re-layouts: 13.2 us -> 1.78 us
    pallas_call x1, Pallas kernels: 102 us -> 104 us  [on_device(): pl.pallas_call(kernel, out_shape=(jax.ShapeDtypeStruct((128, 512), BF16),...]
where the time goes in v2:
time: 109 us
  Pallas kernels  104 us (95%)
  other arithmetic  2.5 us (2%)
  local copies, waits for them, and re-layouts  1.78 us (2%)
    pallas_call x1, Pallas kernels, on_device(): pl.pallas_call(kernel, out_shape=(jax.ShapeDtypeStruct((128, 512), BF16),...  104 us

profile of v2, /device:TPU:7, one launch (start us, length us, event | category | flops | bytes accessed | tf_op | source)
XLA Modules:
  0.0 108.9 jit_solution(18057767908686999246)
XLA Ops:
  0.6 0.0 copy-start.1
  0.6 0.0 copy-start
  0.7 103.9 %shard_map.198 = (bf16[128,512]{1,0:T(8,128)(2,1)}, bf16[128,512]{1,0:T(8,128)(2,1)}, bf16[128,512]{1,0:T(8,128)(2,1)}, f32[64,512]{1,0:T(8,128)}) custom-call(bf16[128,512]{1,0:T(8,128)(2,1)} %q_in.1, bf16[128,512]{1,0:T(8,128)(2,1)} %k_in.1, bf16[128,512]{1,0:T(8,128)(2,1)} %v_in.1, bf16[128,512]{1,0:T(8,128)(2,1)} %z_in.1, bf16[128,512]{1,0:T(8,128)(2,1)} %h_in.1, ...), custom_call_target="tpu_custom_call" | custom-call | tf_op jit(solution)/shard_map/pallas_call | solution.py:378
  104.5 0.0 copy-done.1
  104.6 0.0 copy-done
  104.6 0.0 copy-start.2
  104.6 0.0 copy-start.5
  104.6 0.0 copy-start.6
  104.6 0.0 copy-start.7
  104.6 1.7 %fusion.1 = (bf16[128,512]{1,0:T(8,128)(2,1)}, bf16[128,512]{1,0:T(8,128)(2,1)}) fusion(bf16[128,512]{1,0:T(8,128)(2,1)} %get-tuple-element.12, bf16[128,512]{1,0:T(8,128)(2,1)S(1)} %copy-done, bf16[128,512]{1,0:T(8,128)(2,1)S(1)} %copy-done.1), kind=kLoop, calls=%fused_computation.3 | loop fusion | flops 458752 | bytes 655360 | tf_op jit(solution)/shard_map/convert_element_type | solution.py:436
  106.3 0.0 copy-done.2
  106.3 0.0 copy-done.5
  106.3 0.0 copy-done.6
  106.3 0.0 copy-done.7
  106.4 0.0 copy-start.4
  106.4 0.8 fusion.4
  107.1 0.1 copy-done.4
  107.3 0.0 copy-start.3
  107.3 0.7 copy.24
  107.9 0.3 copy-done.3
  108.2 0.7 copy.25
Async XLA Ops:
  0.6 103.9 %copy-start.1 = (bf16[128,512]{1,0:T(8,128)(2,1)S(1)}, bf16[128,512]{1,0:T(8,128)(2,1)}, u32[]{:S(2)}) copy-start(bf16[128,512]{1,0:T(8,128)(2,1)} %v_in.1) | copy-start | bytes 393220
  0.6 103.9 %copy-start = (bf16[128,512]{1,0:T(8,128)(2,1)S(1)}, bf16[128,512]{1,0:T(8,128)(2,1)}, u32[]{:S(2)}) copy-start(bf16[128,512]{1,0:T(8,128)(2,1)} %k_in.1) | copy-start | bytes 393220
  104.6 1.8 %copy-start.2 = (bf16[64,512]{1,0:T(8,128)(2,1)S(1)}, bf16[64,512]{1,0:T(8,128)(2,1)}, u32[]{:S(2)}) copy-start(bf16[64,512]{1,0:T(8,128)(2,1)} %w_in.1) | copy-start | bytes 196612
  104.6 1.8 %copy-start.5 = (f32[64,512]{1,0:T(8,128)S(1)}, f32[64,512]{1,0:T(8,128)}, u32[]{:S(2)}) copy-start(f32[64,512]{1,0:T(8,128)} %param.22) | copy-start | bytes 393220
  104.6 1.8 %copy-start.6 = (f32[64,512]{1,0:T(8,128)S(1)}, f32[64,512]{1,0:T(8,128)}, u32[]{:S(2)}) copy-start(f32[64,512]{1,0:T(8,128)} %param.23) | copy-start | bytes 393220
  104.6 1.7 %copy-start.7 = (f32[64,512]{1,0:T(8,128)S(1)}, f32[64,512]{1,0:T(8,128)}, u32[]{:S(2)}) copy-start(f32[64,512]{1,0:T(8,128)} %get-tuple-element.14) | copy-start | bytes 393220
  106.4 0.9 copy-start.4
  107.3 1.0 copy-start.3

commit v3 on v2

--- a/solution.py
+++ b/solution.py
@@ -124,9 +124,63 @@
     loads = [pltpu.make_async_copy(src, dst, load.at[i]) for i, (src, dst) in enumerate(pairs)]
     for copy in loads:
         copy.start()
-    for copy in loads[:7]:
+    loads[0].wait()
+    loads[1].wait()
+    pl.semaphore_wait(entry, 76)
+
+    owe("w_s0", wa.at[0, 0], w_s.at[0])
+    owe("w_s1", wa.at[pl.ds(0, 2), 0], w_s.at[1])
+    owe("w_s2", wa.at[pl.ds(0, 4), 0], w_s.at[2])
+    owe("w_s3", wa.at[:, 0], w_s.at[3])
+    owe("w_r3", wa.at[:, 0], w_r.at[3])
+
+    def send_w(block, device, step):
+        return remote(wa.at[block, core], wa.at[block, core], w_s.at[step], w_r.at[step], device)
+
+    send_w(zl, place(z4), 0).start()
+    send_w(zl, sib, 3).start()
+
+    far_copies = []
+    for i in range(4):
+        cols = pl.ds(pl.multiple_of(lax.rem(y + 1 + i, 4) * 128, 128), 128)
+        far_copies.append(remote(g_ref.at[:, cols], gp.at[:, cols], gp_s.at[i], gp_r.at[i], far))
+        far_copies[i].start()
+        owed[f"far_s{i}"] = far_copies[i].wait_send
+        owed[f"far_r{i}"] = far_copies[i].wait_recv
+
+    def spread(src, row, half, i):
+        y_to = lax.rem(y + 1 + i, 4)
+        cols = pl.ds(pl.multiple_of(y_to * 128, 128), 128)
+        for d in range(4):
+            x_to = lax.rem(x + d, 4)
+            if d or i < 3:
+                device = (zl * 8 + y_to * 2 + core, zh * 4 + x_to)
+                remote(src.at[:, cols], ga.at[row, x * 4 + y], grad_s.at[half], grad_r.at[half], device).start()
+            else:
+                ga[row, x * 4 + y] = src[:, cols]
+        if i == 3:
+            owe(f"grad_s{half}", ga.at[0, pl.ds(0, 15)], grad_s.at[half])
+            owe(f"grad_r{half}", ga.at[0, pl.ds(0, 15)], grad_r.at[half])
+
+    for i in range(4):
+        spread(g_ref, zh, 0, i)
+
+    loads[2].wait()
+    loads[3].wait()
+    pa[y] = (q_ref[...].astype(F32) * z_ref[...].astype(F32)).astype(BF16)
+    owe("p_s", pa.at[pl.ds(0, 3)], p_s)
+    owe("p_r", pa.at[pl.ds(0, 3)], p_r)
+    for d in range(1, 4):
+        y_to = lax.rem(y + d, 4)
+        remote(pa.at[y], pa.at[y], p_s, p_r, (zl * 8 + y_to * 2 + core, ch)).start()
+
+    drain(wa.at[0, 0], w_r.at[0])
+    send_w(zl, place(z2), 1).start()
+    send_w(z4, place(z2), 1).start()
+    send_w(z4, sib, 3).start()
+
+    for copy in loads[4:7]:
         copy.wait()
-    pa[y] = (q_ref[...].astype(F32) * z_ref[...].astype(F32)).astype(BF16)
 
     def stage_pair(t, carry):
         cols = pl.ds(pl.multiple_of(t * 128, 128), 128)
@@ -137,47 +191,19 @@
 
     lax.fori_loop(0, 4, stage_pair, 0)
     rkf[ctx] = skf[ctx]
-    pl.semaphore_wait(entry, 76)
-
-    far_copy = remote(g_ref, gp, gp_s, gp_r, far)
-    far_copy.start()
-    owed["far_s"] = far_copy.wait_send
-    owed["far_r"] = far_copy.wait_recv
-    owe("w_s0", wa.at[0, 0], w_s.at[0])
-    owe("w_s1", wa.at[pl.ds(0, 2), 0], w_s.at[1])
-    owe("w_s2", wa.at[pl.ds(0, 4), 0], w_s.at[2])
-    owe("w_s3", wa.at[:, 0], w_s.at[3])
-    owe("w_r3", wa.at[:, 0], w_r.at[3])
-
-    def send_w(block, device, step):
-        return remote(wa.at[block, core], wa.at[block, core], w_s.at[step], w_r.at[step], device)
-
-    send_w(zl, place(z4), 0).start()
-    send_w(zl, sib, 3).start()
-
-    def spread(src, row, half):
-        def body(d, carry):
-            x_to, y_to, device = near(d)
-            cols = pl.ds(pl.multiple_of(y_to * 128, 128), 128)
-            remote(src.at[:, cols], ga.at[row, x * 4 + y], grad_s.at[half], grad_r.at[half], device).start()
-            return carry
-
-        lax.fori_loop(1, 16, body, 0)
-        owe(f"grad_s{half}", ga.at[0, pl.ds(0, 15)], grad_s.at[half])
-        owe(f"grad_r{half}", ga.at[0, pl.ds(0, 15)], grad_r.at[half])
-        ga[row, x * 4 + y] = src[:, pl.ds(pl.multiple_of(y * 128, 128), 128)]
-
-    spread(g_ref, zh, 0)
-    owe("p_s", pa.at[pl.ds(0, 3)], p_s)
-    owe("p_r", pa.at[pl.ds(0, 3)], p_r)
-    for d in range(1, 4):
-        y_to = lax.rem(y + d, 4)
-        remote(pa.at[y], pa.at[y], p_s, p_r, (zl * 8 + y_to * 2 + core, ch)).start()
-
-    drain(wa.at[0, 0], w_r.at[0])
-    send_w(zl, place(z2), 1).start()
-    send_w(z4, place(z2), 1).start()
-    send_w(z4, sib, 3).start()
+
+    def send_pair(d, carry):
+        to = lax.rem(ctx + d, 64)
+        remote(skf.at[to], rkf.at[ctx], kf_s, kf_r, (to, ch)).start()
+        return carry
+
+    lax.fori_loop(1, 64, send_pair, 0)
+    owe("kf_s", skf.at[pl.ds(0, 63)], kf_s)
+    owe("kf_r", rkf.at[pl.ds(0, 63)], kf_r)
+    for i in range(2):
+        settle(f"far_r{i}")
+        spread(gp, 1 - zh, 1, i)
+
     drain(wa.at[pl.ds(0, 2), 0], w_r.at[1])
     z24 = lax.rem(z2 + 4, 8)
     for block in (zl, z4, z2, z24):
@@ -185,44 +211,11 @@
     send_w(z2, sib, 3).start()
     send_w(z24, sib, 3).start()
 
-    settle("far_r")
-    spread(gp, 1 - zh, 1)
-
-    def send_pair(d, carry):
-        to = lax.rem(ctx + d, 64)
-        remote(skf.at[to], rkf.at[ctx], kf_s, kf_r, (to, ch)).start()
-        return carry
-
-    lax.fori_loop(1, 64, send_pair, 0)
-    owe("kf_s", skf.at[pl.ds(0, 63)], kf_s)
-    owe("kf_r", rkf.at[pl.ds(0, 63)], kf_r)
-
-    drain(wa.at[pl.ds(0, 4), 0], w_r.at[2])
-    for block in (z1, lax.rem(z1 + 4, 8), z1 + 2 - 4 * ((z1 // 2) % 2), lax.rem(z1 + 6 - 4 * ((z1 // 2) % 2), 8)):
-        send_w(block, sib, 3).start()
-    settle("w_r3")
-    settle("grad_r0")
-
-    acc1[...] = jnp.zeros_like(acc1)
-
-    def multiply(row):
-        def body(t, carry):
-            left = ga[row, pl.ds(t * 4, 4)].reshape(512, 128)
-            right = wa[row * 4 + t].reshape(128, 512)
-            acc1[...] += jnp.dot(left, right, preferred_element_type=F32)
-            return carry
-
-        lax.fori_loop(0, 4, body, 0)
-
-    multiply(zh)
-    settle("grad_r1")
-    multiply(1 - zh)
-    owe("one_s", s1, one_s)
-    owe("one_r", r1, one_r)
-    for d in range(1, 4):
-        y_to = lax.rem(y + d, 4)
-        s1[d - 1] = acc1[pl.ds(pl.multiple_of(y_to * 128, 128), 128), :].astype(BF16)
-        remote(s1.at[d - 1], r1.at[d - 1], one_s, one_r, (zl * 8 + y_to * 2 + core, ch)).start()
+    for i in range(2, 4):
+        settle(f"far_r{i}")
+        spread(gp, 1 - zh, 1, i)
+
+    settle("grad_r0", "grad_r1")
 
     settle("p_r")
     first_core = core == 0
@@ -242,23 +235,9 @@
     core_copy.start()
     owed["core_s"], owed["core_r"] = core_copy.wait_send, core_copy.wait_recv
 
-    settle("one_r")
-    delta = acc1[pl.ds(pl.multiple_of(y * 128, 128), 128), :]
-    for d in range(3):
-        delta = delta + r1[d].astype(F32)
-    qg_ref[...] = (delta * z_ref[...].astype(F32)).astype(BF16)
-    conv = (delta * q_ref[...].astype(F32)).astype(BF16).astype(F32)
-    sg[...] = conv.T.reshape(32, 16, 128).astype(BF16)
-    rg[core, chip] = sg[chip]
-
-    def send_conv(d, carry):
-        to = lax.rem(chip + d, 32)
-        remote(sg.at[to], rg.at[core, chip], g_s.at[0], g_r.at[0], (to * 2 + core, ch)).start()
-        return carry
-
-    lax.fori_loop(1, 32, send_conv, 0)
-    owe("g_s", sg.at[pl.ds(0, 31)], g_s.at[0])
-    owe("g_r", rg.at[0, pl.ds(0, 31)], g_r.at[0])
+    drain(wa.at[pl.ds(0, 4), 0], w_r.at[2])
+    for block in (z1, lax.rem(z1 + 4, 8), z1 + 2 - 4 * ((z1 // 2) % 2), lax.rem(z1 + 6 - 4 * ((z1 // 2) % 2), 8)):
+        send_w(block, sib, 3).start()
 
     settle("core_r")
     bit0, bit1, bit2 = zl % 2, (zl // 2) % 2, zl // 4
@@ -269,6 +248,65 @@
     a_copy = remote(sa, ra, two_s.at[1], two_r.at[1], place(z1))
     a_copy.start()
     owed["a_s"], owed["a_r"] = a_copy.wait_send, a_copy.wait_recv
+
+    settle("w_r3")
+
+    acc1[...] = jnp.zeros_like(acc1)
+
+    def multiply(row):
+        def body(t, carry):
+            left = ga[row, pl.ds(t * 4, 4)].reshape(512, 128)
+            right = wa[row * 4 + t].reshape(128, 512)
+            acc1[...] += jnp.dot(left, right, preferred_element_type=F32)
+            return carry
+
+        lax.fori_loop(0, 4, body, 0)
+
+    multiply(zh)
+    multiply(1 - zh)
+    owe("one_s", s1, one_s)
+    owe("one_r", r1, one_r)
+    for d in range(1, 4):
+        y_to = lax.rem(y + d, 4)
+        s1[d - 1] = acc1[pl.ds(pl.multiple_of(y_to * 128, 128), 128), :].astype(BF16)
+        remote(s1.at[d - 1], r1.at[d - 1], one_s, one_r, (zl * 8 + y_to * 2 + core, ch)).start()
+
+
+    settle("a_r")
+    for i in range(2):
+        give, keep = 2 * i + 1 - bit1, 2 * i + bit1
+        sb[i] = (acc2[2 * give + bit0] + ra[give].astype(F32)).astype(BF16)
+        acc2[2 * keep + bit0] = acc2[2 * keep + bit0] + ra[keep].astype(F32)
+    b_copy = remote(sb, rb, two_s.at[2], two_r.at[2], place(z2))
+    b_copy.start()
+    owed["b_s"], owed["b_r"] = b_copy.wait_send, b_copy.wait_recv
+
+    settle("one_r")
+    delta = acc1[pl.ds(pl.multiple_of(y * 128, 128), 128), :]
+    for d in range(3):
+        delta = delta + r1[d].astype(F32)
+    qg_ref[...] = (delta * z_ref[...].astype(F32)).astype(BF16)
+    conv = (delta * q_ref[...].astype(F32)).astype(BF16).astype(F32)
+    sg[...] = conv.T.reshape(32, 16, 128).astype(BF16)
+    rg[core, chip] = sg[chip]
+
+    def send_conv(d, carry):
+        to = lax.rem(chip + d, 32)
+        remote(sg.at[to], rg.at[core, chip], g_s.at[0], g_r.at[0], (to * 2 + core, ch)).start()
+        return carry
+
+    lax.fori_loop(1, 32, send_conv, 0)
+    owe("g_s", sg.at[pl.ds(0, 31)], g_s.at[0])
+    owe("g_r", rg.at[0, pl.ds(0, 31)], g_r.at[0])
+
+    settle("b_r")
+    give, keep = 1 - bit2, bit2
+    sd[...] = (acc2[4 * give + 2 * bit1 + bit0] + rb[give].astype(F32)).astype(BF16)
+    d_copy = remote(sd, rd, two_s.at[3], two_r.at[3], place(z4))
+    d_copy.start()
+    owed["d_s"], owed["d_r"] = d_copy.wait_send, d_copy.wait_recv
+    mine = acc2[4 * keep + 2 * bit1 + bit0] + rb[keep].astype(F32)
+    wg_ref[...] = mine
 
     for copy in loads[7:]:
         copy.wait()
@@ -291,28 +329,10 @@
     spectrum(0, first_ref, 0)
     spectrum(8, first_ref, 1)
 
-    settle("a_r")
-    for i in range(2):
-        give, keep = 2 * i + 1 - bit1, 2 * i + bit1
-        sb[i] = (acc2[2 * give + bit0] + ra[give].astype(F32)).astype(BF16)
-        acc2[2 * keep + bit0] = acc2[2 * keep + bit0] + ra[keep].astype(F32)
-    b_copy = remote(sb, rb, two_s.at[2], two_r.at[2], place(z2))
-    b_copy.start()
-    owed["b_s"], owed["b_r"] = b_copy.wait_send, b_copy.wait_recv
-
     settle("g_r")
     g_copy = remote(rg.at[core], rg.at[core], g_s.at[1], g_r.at[1], sib)
     g_copy.start()
     owed["gs_s"], owed["gs_r"] = g_copy.wait_send, g_copy.wait_recv
-
-    settle("b_r")
-    give, keep = 1 - bit2, bit2
-    sd[...] = (acc2[4 * give + 2 * bit1 + bit0] + rb[give].astype(F32)).astype(BF16)
-    d_copy = remote(sd, rd, two_s.at[3], two_r.at[3], place(z4))
-    d_copy.start()
-    owed["d_s"], owed["d_r"] = d_copy.wait_send, d_copy.wait_recv
-    mine = acc2[4 * keep + 2 * bit1 + bit0] + rb[keep].astype(F32)
-    wg_ref[...] = mine
 
     settle("gs_r")
     fs[...] = rg[...].astype(F32).reshape(1024, 128)
@@ -416,7 +436,7 @@
             full(3, 8 * HALF, 256),
             full(2 * HALF, 1024),
             dma((2,)), dma((2,)),
-            dma, dma,
+            dma((4,)), dma((4,)),
             dma((4,)), dma((4,)),
             dma, dma,
             dma, dma,

time: 109 us -> 101 us (0.927); the launches traced: 109 us -> 99.7 us
  Pallas kernels: 104 us -> 94.7 us
    pallas_call x1, Pallas kernels: 104 us -> 94.7 us  [on_device(): pl.pallas_call(kernel, out_shape=(jax.ShapeDtypeStruct((128, 512), BF16),...]
where the time goes in v3:
time: 101 us; the launch traced here: 99.7 us
  Pallas kernels  94.7 us (94%)
  other arithmetic  2.5 us (2%)
  local copies, waits for them, and re-layouts  1.78 us (2%)
    pallas_call x1, Pallas kernels, on_device(): pl.pallas_call(kernel, out_shape=(jax.ShapeDtypeStruct((128, 512), BF16),...  94.7 us

profile of v3, /device:TPU:7, one launch (start us, length us, event | category | flops | bytes accessed | tf_op | source)
XLA Modules:
  0.0 99.7 jit_solution(9377241985660662566)
XLA Ops:
  0.6 0.0 copy-start.1
  0.6 0.0 copy-start
  0.7 94.7 %shard_map.198 = (bf16[128,512]{1,0:T(8,128)(2,1)}, bf16[128,512]{1,0:T(8,128)(2,1)}, bf16[128,512]{1,0:T(8,128)(2,1)}, f32[64,512]{1,0:T(8,128)}) custom-call(bf16[128,512]{1,0:T(8,128)(2,1)} %q_in.1, bf16[128,512]{1,0:T(8,128)(2,1)} %k_in.1, bf16[128,512]{1,0:T(8,128)(2,1)} %v_in.1, bf16[128,512]{1,0:T(8,128)(2,1)} %z_in.1, bf16[128,512]{1,0:T(8,128)(2,1)} %h_in.1, ...), custom_call_target="tpu_custom_call" | custom-call | tf_op jit(solution)/shard_map/pallas_call | solution.py:398
  95.4 0.0 copy-done.1
  95.4 0.0 copy-done
  95.4 0.0 copy-start.2
  95.4 0.0 copy-start.5
  95.4 0.0 copy-start.6
  95.4 0.0 copy-start.7
  95.4 1.7 %fusion.1 = (bf16[128,512]{1,0:T(8,128)(2,1)}, bf16[128,512]{1,0:T(8,128)(2,1)}) fusion(bf16[128,512]{1,0:T(8,128)(2,1)} %get-tuple-element.12, bf16[128,512]{1,0:T(8,128)(2,1)S(1)} %copy-done, bf16[128,512]{1,0:T(8,128)(2,1)S(1)} %copy-done.1), kind=kLoop, calls=%fused_computation.3 | loop fusion | flops 458752 | bytes 655360 | tf_op jit(solution)/shard_map/convert_element_type | solution.py:456
  97.2 0.0 copy-done.2
  97.2 0.0 copy-done.5
  97.2 0.0 copy-done.6
  97.2 0.0 copy-done.7
  97.2 0.0 copy-start.4
  97.2 0.8 fusion.4
  98.0 0.1 copy-done.4
  98.1 0.0 copy-start.3
  98.1 0.7 copy.24
  98.8 0.3 copy-done.3
  99.1 0.7 copy.25
Async XLA Ops:
  0.6 94.7 %copy-start.1 = (bf16[128,512]{1,0:T(8,128)(2,1)S(1)}, bf16[128,512]{1,0:T(8,128)(2,1)}, u32[]{:S(2)}) copy-start(bf16[128,512]{1,0:T(8,128)(2,1)} %v_in.1) | copy-start | bytes 393220
  0.6 94.7 %copy-start = (bf16[128,512]{1,0:T(8,128)(2,1)S(1)}, bf16[128,512]{1,0:T(8,128)(2,1)}, u32[]{:S(2)}) copy-start(bf16[128,512]{1,0:T(8,128)(2,1)} %k_in.1) | copy-start | bytes 393220
  95.4 1.8 %copy-start.2 = (bf16[64,512]{1,0:T(8,128)(2,1)S(1)}, bf16[64,512]{1,0:T(8,128)(2,1)}, u32[]{:S(2)}) copy-start(bf16[64,512]{1,0:T(8,128)(2,1)} %w_in.1) | copy-start | bytes 196612
  95.4 1.8 %copy-start.5 = (f32[64,512]{1,0:T(8,128)S(1)}, f32[64,512]{1,0:T(8,128)}, u32[]{:S(2)}) copy-start(f32[64,512]{1,0:T(8,128)} %param.22) | copy-start | bytes 393220
  95.4 1.8 %copy-start.6 = (f32[64,512]{1,0:T(8,128)S(1)}, f32[64,512]{1,0:T(8,128)}, u32[]{:S(2)}) copy-start(f32[64,512]{1,0:T(8,128)} %param.23) | copy-start | bytes 393220
  95.4 1.7 %copy-start.7 = (f32[64,512]{1,0:T(8,128)S(1)}, f32[64,512]{1,0:T(8,128)}, u32[]{:S(2)}) copy-start(f32[64,512]{1,0:T(8,128)} %get-tuple-element.14) | copy-start | bytes 393220
  97.2 0.9 copy-start.4
  98.1 1.0 copy-start.3

commit v4 on v3

--- a/solution.py
+++ b/solution.py
@@ -285,7 +285,6 @@
     delta = acc1[pl.ds(pl.multiple_of(y * 128, 128), 128), :]
     for d in range(3):
         delta = delta + r1[d].astype(F32)
-    qg_ref[...] = (delta * z_ref[...].astype(F32)).astype(BF16)
     conv = (delta * q_ref[...].astype(F32)).astype(BF16).astype(F32)
     sg[...] = conv.T.reshape(32, 16, 128).astype(BF16)
     rg[core, chip] = sg[chip]
@@ -296,6 +295,7 @@
         return carry
 
     lax.fori_loop(1, 32, send_conv, 0)
+    qg_ref[...] = (delta * z_ref[...].astype(F32)).astype(BF16)
     owe("g_s", sg.at[pl.ds(0, 31)], g_s.at[0])
     owe("g_r", rg.at[0, pl.ds(0, 31)], g_r.at[0])
 

time: 101 us -> 102 us (level)
  no operation moved by 1% of the time
where the time goes in v4:
time: 102 us; the launch traced here: 99.8 us
  Pallas kernels  94.8 us (93%)
  other arithmetic  2.5 us (2%)
  local copies, waits for them, and re-layouts  1.78 us (2%)
    pallas_call x1, Pallas kernels, on_device(): pl.pallas_call(kernel, out_shape=(jax.ShapeDtypeStruct((128, 512), BF16),...  94.8 us

profile of v4, /device:TPU:7, one launch (start us, length us, event | category | flops | bytes accessed | tf_op | source)
XLA Modules:
  0.0 99.8 jit_solution(5916268101499347949)
XLA Ops:
  0.6 0.0 copy-start.1
  0.6 0.0 copy-start
  0.7 94.8 %shard_map.198 = (bf16[128,512]{1,0:T(8,128)(2,1)}, bf16[128,512]{1,0:T(8,128)(2,1)}, bf16[128,512]{1,0:T(8,128)(2,1)}, f32[64,512]{1,0:T(8,128)}) custom-call(bf16[128,512]{1,0:T(8,128)(2,1)} %q_in.1, bf16[128,512]{1,0:T(8,128)(2,1)} %k_in.1, bf16[128,512]{1,0:T(8,128)(2,1)} %v_in.1, bf16[128,512]{1,0:T(8,128)(2,1)} %z_in.1, bf16[128,512]{1,0:T(8,128)(2,1)} %h_in.1, ...), custom_call_target="tpu_custom_call" | custom-call | tf_op jit(solution)/shard_map/pallas_call | solution.py:398
  95.4 0.0 copy-done.1
  95.4 0.0 copy-done
  95.4 0.0 copy-start.2
  95.4 0.0 copy-start.5
  95.5 0.0 copy-start.6
  95.5 0.0 copy-start.7
  95.5 1.7 %fusion.1 = (bf16[128,512]{1,0:T(8,128)(2,1)}, bf16[128,512]{1,0:T(8,128)(2,1)}) fusion(bf16[128,512]{1,0:T(8,128)(2,1)} %get-tuple-element.12, bf16[128,512]{1,0:T(8,128)(2,1)S(1)} %copy-done, bf16[128,512]{1,0:T(8,128)(2,1)S(1)} %copy-done.1), kind=kLoop, calls=%fused_computation.3 | loop fusion | flops 458752 | bytes 655360 | tf_op jit(solution)/shard_map/convert_element_type | solution.py:456
  97.2 0.0 copy-done.2
  97.2 0.0 copy-done.5
  97.2 0.0 copy-done.6
  97.2 0.0 copy-done.7
  97.2 0.0 copy-start.4
  97.2 0.8 fusion.4
  98.0 0.1 copy-done.4
  98.2 0.0 copy-start.3
  98.2 0.7 copy.24
  98.8 0.3 copy-done.3
  99.1 0.7 copy.25
Async XLA Ops:
  0.6 94.8 %copy-start.1 = (bf16[128,512]{1,0:T(8,128)(2,1)S(1)}, bf16[128,512]{1,0:T(8,128)(2,1)}, u32[]{:S(2)}) copy-start(bf16[128,512]{1,0:T(8,128)(2,1)} %v_in.1) | copy-start | bytes 393220
  0.6 94.8 %copy-start = (bf16[128,512]{1,0:T(8,128)(2,1)S(1)}, bf16[128,512]{1,0:T(8,128)(2,1)}, u32[]{:S(2)}) copy-start(bf16[128,512]{1,0:T(8,128)(2,1)} %k_in.1) | copy-start | bytes 393220
  95.4 1.8 %copy-start.2 = (bf16[64,512]{1,0:T(8,128)(2,1)S(1)}, bf16[64,512]{1,0:T(8,128)(2,1)}, u32[]{:S(2)}) copy-start(bf16[64,512]{1,0:T(8,128)(2,1)} %w_in.1) | copy-start | bytes 196612
  95.4 1.8 %copy-start.5 = (f32[64,512]{1,0:T(8,128)S(1)}, f32[64,512]{1,0:T(8,128)}, u32[]{:S(2)}) copy-start(f32[64,512]{1,0:T(8,128)} %param.22) | copy-start | bytes 393220
  95.5 1.8 %copy-start.6 = (f32[64,512]{1,0:T(8,128)S(1)}, f32[64,512]{1,0:T(8,128)}, u32[]{:S(2)}) copy-start(f32[64,512]{1,0:T(8,128)} %param.23) | copy-start | bytes 393220
  95.5 1.7 %copy-start.7 = (f32[64,512]{1,0:T(8,128)S(1)}, f32[64,512]{1,0:T(8,128)}, u32[]{:S(2)}) copy-start(f32[64,512]{1,0:T(8,128)} %get-tuple-element.14) | copy-start | bytes 393220
  97.2 0.9 copy-start.4
  98.2 1.0 copy-start.3
